TPU v7x, 32 devices: a whole 2x2x4 slice. The times are simulated.
32 devices in a mesh: sec: 4 (over y, x), tile: 4 (over z), half: 2 (over core).
Axes of the slice: x: 2, y: 2, z: 4, core: 2. Of those that a mesh axis runs over, the one named last changes fastest.
Arguments:
- sections_in: bfloat16 [8, 256, 1024], P('sec', 'tile', 'half'), parts along dimension 2, may hold values from -30 to 30
- first_kernel: bfloat16 [12, 1, 3, 3, 3], replicated, may hold values from -1.25 to 1.25
- first_bias: float32 [12], replicated, may hold values from -3 to 3
- second_kernel: bfloat16 [12, 12, 3, 3, 3], replicated, may hold values from -0.3125 to 0.3125
- second_bias: float32 [12], replicated, may hold values from -3 to 3
- head_kernel: bfloat16 [3, 12], replicated, may hold values from -1.75 to 1.75
- head_bias: float32 [3], replicated, may hold values from -3 to 3
Outputs:
- affinity: float32 [3, 8, 256, 1024], P(None, None, 'sec', ('half', 'tile')), parts along dimension 3
There are 2 independent parts, one for each index of `half`. A program takes and returns all parts, laid end to end along the dimension named above; an argument that names none is the same for every part. Nothing has to cross between parts.
All inputs are finite; a program needn't handle non-finite values.
Results may differ from a plain program's by a relative error of at most 0.0016.
Values may be sent and summed in bfloat16 or wider, within the bound.
A program may use at most 128 MiB of HBM per device.

v0:
```python
import jax
import jax.numpy as jnp
from jax import lax
from jax.sharding import PartitionSpec as P


def padded_2(shard, sides, width):
    for axis, dim in sides:
        peers, length = (lax.axis_size(axis), shard.shape[dim])
        up = [(i, (i + 1) % peers) for i in range(peers - 1)]
        down = [(j, i) for i, j in up]
        last = lax.slice_in_dim(shard, length - width, length, axis=dim)
        initial = lax.slice_in_dim(shard, 0, width, axis=dim)
        before = lax.ppermute(last, axis, up)
        after = lax.ppermute(initial, axis, down)
        shard = jnp.concatenate([before, shard, after], axis=dim)
    return shard


def convolve(volume, kernel, padding):
    return lax.conv_general_dilated(
        volume,
        kernel,
        (1, 1, 1),
        padding,
        dimension_numbers=("NCDHW", "OIDHW", "NCDHW"),
        preferred_element_type=jnp.float32,
    )


def activate(summed, bias):
    return jax.nn.relu(summed + bias[None, :, None, None, None]).astype(jnp.bfloat16)


def local_sums(volume):
    values = volume.astype(jnp.float32)
    return (jnp.sum(values, axis=(1, 2)), jnp.sum(values * values, axis=(1, 2)))


def normalize(volume, first_sum, second_sum, cells_total):
    average = first_sum / cells_total
    variance = second_sum / cells_total - average * average
    inv_std = lax.rsqrt(variance + 1e-05)
    shifted = volume.astype(jnp.float32) - average[:, None, None]
    return (shifted * inv_std[:, None, None]).astype(jnp.bfloat16)


def brick_normalize(volume):
    plain_sum, square_sum = local_sums(volume)
    first_sum, second_sum = lax.psum((plain_sum, square_sum), ("sec", "tile"))
    cells_total = volume.shape[1] * volume.shape[2] * lax.axis_size("sec") * lax.axis_size("tile")
    return normalize(volume, first_sum, second_sum, cells_total)


def regroup(volume):
    return lax.all_to_all(
        lax.all_to_all(volume, "tile", split_axis=2, concat_axis=1, tiled=True),
        "sec",
        split_axis=1,
        concat_axis=0,
        tiled=True,
    )


def finish(widened, second_kernel, second_bias, head_kernel, head_bias):
    second_out = activate(
        convolve(widened[None], second_kernel, ((1, 1), (0, 0), (0, 0))), second_bias
    )
    logits = jnp.einsum(
        "oc,czyx->ozyx", head_kernel, second_out[0], preferred_element_type=jnp.float32
    )
    return jax.nn.sigmoid(logits + head_bias[:, None, None, None])


def per_device(
    sections_in, first_kernel, first_bias, second_kernel, second_bias, head_kernel, head_bias
):
    level = ((1, 1), (0, 0), (0, 0))
    brick = brick_normalize(regroup(sections_in))
    padded = padded_2(brick, (("sec", 1), ("tile", 2)), 2)
    first_out = activate(convolve(padded[None, None], first_kernel, level), first_bias)[0]
    rows_here = brick.shape[1]
    cols_here = brick.shape[2]
    row_index = lax.axis_index("sec") * rows_here - 1 + jnp.arange(rows_here + 2, dtype=jnp.int32)
    col_index = lax.axis_index("tile") * cols_here - 1 + jnp.arange(cols_here + 2, dtype=jnp.int32)
    row_inside = (row_index >= 0) & (row_index < rows_here * lax.axis_size("sec"))
    col_inside = (col_index >= 0) & (col_index < cols_here * lax.axis_size("tile"))
    inside = row_inside[:, None] & col_inside[None, :]
    widened = jnp.where(inside[None, None], first_out, jnp.zeros((), jnp.bfloat16))
    return finish(widened, second_kernel, second_bias, head_kernel, head_bias)


def solution(mesh):
    in_specs = (P("sec", "tile", "half"), P(), P(), P(), P(), P(), P())
    out_specs = P(None, None, "sec", ("half", "tile"))
    return jax.shard_map(
        per_device, mesh=mesh, in_specs=in_specs, out_specs=out_specs, check_vma=False
    )
```

profile of v0, /device:TPU:0, one launch (start us, length us, event | category | flops | bytes accessed | tf_op | source)
XLA Modules:
  0.0 273.2 jit_solution(5084673572646575382)
XLA Ops:
  0.0 0.0 copy-start
  0.0 1.1 copy.95
  1.1 0.9 reshape.84
  2.0 6.3 %all-to-all-start = ((bf16[4,2,8192]{2,1,0:T(2,128)(2,1)}), bf16[4,2,8192]{2,1,0:T(2,128)(2,1)S(1)}, u32[]{:S(2)}, u32[]{:S(2)}) async-start(bf16[4,2,8192]{2,1,0:T(2,128)(2,1)} %reshape.84), calls=%async_computation | async-start | bytes 262144 | tf_op jit(solution)/shard_map/all_to_all | solution.py:57
  8.3 6.1 %all-to-all-done = bf16[4,2,8192]{2,1,0:T(2,128)(2,1)S(1)} async-done(((bf16[4,2,8192]{2,1,0:T(2,128)(2,1)}), bf16[4,2,8192]{2,1,0:T(2,128)(2,1)S(1)}, u32[]{:S(2)}, u32[]{:S(2)}) %all-to-all-start) | async-done | bytes 131104 | tf_op jit(solution)/shard_map/all_to_all | solution.py:57
  14.4 0.2 reshape.85
  14.6 0.2 copy.116
  14.8 0.8 copy.98
  15.6 3.7 %all-to-all-start.1 = ((bf16[2,256,128]{2,0,1:T(2,128)(2,1)}), bf16[2,256,128]{2,0,1:T(2,128)(2,1)S(1)}, u32[]{:S(2)}, u32[]{:S(2)}) async-start(bf16[2,256,128]{2,0,1:T(2,128)(2,1)} %copy.98), calls=%async_computation.1 | async-start | bytes 262144 | tf_op jit(solution)/shard_map/all_to_all | solution.py:56
  19.3 5.0 %all-to-all-done.1 = bf16[2,256,128]{2,0,1:T(2,128)(2,1)S(1)} async-done(((bf16[2,256,128]{2,0,1:T(2,128)(2,1)}), bf16[2,256,128]{2,0,1:T(2,128)(2,1)S(1)}, u32[]{:S(2)}, u32[]{:S(2)}) %all-to-all-start.1) | async-done | bytes 131104 | tf_op jit(solution)/shard_map/all_to_all | solution.py:56
  24.4 0.1 fusion.37
  24.6 0.1 copy.101
  24.6 0.1 reduce_sum.23
  24.7 0.1 copy.102
  24.8 0.1 reduce_sum.25
  24.9 38.3 %all-reduce = (f32[8]{0:T(128)S(1)}, f32[8]{0:T(128)S(1)}) all-reduce(f32[8]{0:T(128)S(1)} %reduce_sum.25, f32[8]{0:T(128)S(1)} %reduce_sum.23), channel_id=1, replica_groups=mesh['sec'=4,'tile'=4,'half'=2] {'sec','tile'}, use_global_device_ids=true, to_apply=%region_3.0 | all-reduce | flops 16 | bytes 128 | tf_op jit(solution)/shard_map/psum | solution.py:50
  63.3 0.1 fusion.36
  63.4 1.3 collective-permute-start
  64.7 1.3 collective-permute-start.1
  66.0 0.0 collective-permute-done
  66.0 5.9 %collective-permute-done.1 = bf16[8,2,128]{2,1,0:T(2,128)(2,1)S(1)} collective-permute-done((bf16[8,2,128]{2,1,0:T(2,128)(2,1)S(1)}, bf16[8,2,128]{2,1,0:T(2,128)(2,1)S(1)}, u32[]{:S(2)}, u32[]{:S(2)}) %collective-permute-start.1) | collective-permute-done | bytes 4128 | tf_op jit(solution)/shard_map/ppermute | solution.py:15
  71.9 0.1 pad_maximum_fusion
  72.0 0.1 fusion.44
  72.1 1.6 collective-permute-start.2
  73.7 1.3 collective-permute-start.3
  75.0 0.1 broadcast_and_fusion
  75.1 1.3 collective-permute-done.2
  76.4 4.4 %collective-permute-done.3 = bf16[8,68,2]{2,1,0:T(8,128)(2,1)S(1)} collective-permute-done((bf16[8,68,2]{2,1,0:T(8,128)(2,1)S(1)}, bf16[8,68,2]{2,1,0:T(8,128)(2,1)S(1)}, u32[]{:S(2)}, u32[]{:S(2)}) %collective-permute-start.3) | collective-permute-done | bytes 2208 | tf_op jit(solution)/shard_map/ppermute | solution.py:15
  80.7 0.3 maximum_bitcast_fusion
  81.0 0.3 copy.120
  81.3 0.1 pad.clone
  81.4 0.1 fusion.34
  81.4 10.0 %copy.105 = bf16[1,8,68,8,19]{3,0,4,2,1:T(2,128)(2,1)} copy(bf16[1,8,68,8,19]{2,1,4,3,0:T(8,128)(2,1)S(1)} %fusion.34) | data formatting | bytes 330752 | tf_op jit(solution)/shard_map/conv_general_dilated | solution.py:21
  91.4 62.1 %maximum_convert_fusion = bf16[8,66,8,17,12]{4,2,3,1,0:T(8,128)(2,1)} fusion(f32[12]{0:T(128)} %param.9, pred[8,17]{0,1:T(8,128)(4,1)} %constant.50, bf16[1,8,68,8,19]{3,0,4,2,1:T(2,128)(2,1)} %copy.105, bf16[12,1,3,3,3]{0,4,3,2,1:T(4,128)(2,1)} %param.8), kind=kOutput, calls=%fused_computation.2 | convolution fusion | flops 46100736 | bytes 1889600 | tf_op jit(solution)/shard_map/conv_general_dilated | solution.py:21
  153.5 18.6 %copy.107 = bf16[8,66,8,17,12]{1,0,4,3,2:T(8,128)(2,1)S(1)} copy(bf16[8,66,8,17,12]{4,2,3,1,0:T(8,128)(2,1)} %maximum_convert_fusion) | data formatting | bytes 3446784 | tf_op jit(solution)/shard_map/convert_element_type | solution.py:32
  172.2 0.3 fusion.11
  172.4 0.0 copy-start.2
  172.5 0.0 copy-start.4
  172.5 0.5 copy.121
  173.0 0.8 pad.2.clone
  173.9 16.7 %copy.110 = bf16[12,8,66,1,8,17]{0,4,5,2,1,3:T(8,128)(2,1)} copy(bf16[12,8,66,1,8,17]{2,1,5,4,0,3:T(8,128)(2,1)S(1)} %bitcast.62) | data formatting | bytes 3446784 | tf_op jit(solution)/shard_map/conv_general_dilated | solution.py:21
  190.5 2.2 slice.26
  192.8 50.5 %maximum_convert_fusion.1 = bf16[8,64,8,17,12]{4,2,3,1,0:T(8,128)(2,1)} fusion(f32[12]{0:T(128)S(1)} %copy-done.2, pred[8,17]{0,1:T(8,128)(4,1)S(1)} %copy-done.4, bf16[12,8,66,1,7,2]{0,4,5,2,1,3:T(8,128)(2,1)S(1)} %slice.26, bf16[12,8,66,1,8,17]{0,4,5,2,1,3:T(8,128)(2,1)} %copy.110, bf16[12,12,3,3,3]{1,4,3,2,0:T(4,128)(2,1)S(1)} %copy-done), kind=kOutput, calls=%fused_computation.3 | convolution fusion | flops 505457664 | bytes 3579928 | tf_op jit(solution)/shard_map/conv_general_dilated | solution.py:21
  243.3 18.9 %copy.112 = bf16[8,64,8,17,12]{1,0,4,3,2:T(8,128)(2,1)S(1)} copy(bf16[8,64,8,17,12]{4,2,3,1,0:T(8,128)(2,1)} %maximum_convert_fusion.1) | data formatting | bytes 3342336 | tf_op jit(solution)/shard_map/convert_element_type | solution.py:32
  262.2 1.8 slice.27
  264.0 7.5 %copy.119 = bf16[8,64,1,128,12]{3,4,1,0,2:T(8,128)(2,1)S(1)} copy(bf16[8,64,1,128,12]{1,0,4,3,2:T(8,128)(2,1)} %slice.27) | data formatting | bytes 3145728
  271.6 0.7 fusion.29
  272.3 1.0 copy.114
  (15 shorter events, 0.1 us)
Async XLA Ops:
  0.0 192.7 %copy-start = (bf16[12,12,3,3,3]{1,4,3,2,0:T(4,128)(2,1)S(1)}, bf16[12,12,3,3,3]{1,4,3,2,0:T(4,128)(2,1)}, u32[]{:S(2)}) copy-start(bf16[12,12,3,3,3]{1,4,3,2,0:T(4,128)(2,1)} %param.10) | copy-start | bytes 23332
  2.0 12.4 %all-to-all-start = ((bf16[4,2,8192]{2,1,0:T(2,128)(2,1)}), bf16[4,2,8192]{2,1,0:T(2,128)(2,1)S(1)}, u32[]{:S(2)}, u32[]{:S(2)}) async-start(bf16[4,2,8192]{2,1,0:T(2,128)(2,1)} %reshape.84), calls=%async_computation | async-start | bytes 262144 | tf_op jit(solution)/shard_map/all_to_all | solution.py:57
  15.6 8.7 %all-to-all-start.1 = ((bf16[2,256,128]{2,0,1:T(2,128)(2,1)}), bf16[2,256,128]{2,0,1:T(2,128)(2,1)S(1)}, u32[]{:S(2)}, u32[]{:S(2)}) async-start(bf16[2,256,128]{2,0,1:T(2,128)(2,1)} %copy.98), calls=%async_computation.1 | async-start | bytes 262144 | tf_op jit(solution)/shard_map/all_to_all | solution.py:56
  63.4 2.6 collective-permute-start
  64.7 7.2 %collective-permute-start.1 = (bf16[8,2,128]{2,1,0:T(2,128)(2,1)S(1)}, bf16[8,2,128]{2,1,0:T(2,128)(2,1)S(1)}, u32[]{:S(2)}, u32[]{:S(2)}) collective-permute-start(bf16[8,2,128]{2,1,0:T(2,128)(2,1)S(1)} %get-tuple-element.12), channel_id=1, source_target_pairs={{8,0},{16,8},{24,16},{9,1},{17,9},{25,17},{10,2},{18,10},{26,18},{... | collective-permute-start | bytes 12296 | tf_op jit(solution)/shard_map/ppermute | solution.py:15
  72.1 4.2 %collective-permute-start.2 = (bf16[8,68,2]{2,1,0:T(8,128)(2,1)S(1)}, bf16[8,68,2]{2,1,0:T(8,128)(2,1)S(1)}, u32[]{:S(2)}, u32[]{:S(2)}) collective-permute-start(bf16[8,68,2]{2,1,0:T(8,128)(2,1)S(1)} %get-tuple-element.9), channel_id=1, source_target_pairs={{0,2},{2,4},{4,6},{1,3},{3,5},{5,7},{8,10},{10,12},{12,14},{9,11},... | collective-permute-start | bytes 6536 | tf_op jit(solution)/shard_map/ppermute | solution.py:14
  73.7 7.0 %collective-permute-start.3 = (bf16[8,68,2]{2,1,0:T(8,128)(2,1)S(1)}, bf16[8,68,2]{2,1,0:T(8,128)(2,1)S(1)}, u32[]{:S(2)}, u32[]{:S(2)}) collective-permute-start(bf16[8,68,2]{2,1,0:T(8,128)(2,1)S(1)} %get-tuple-element.10), channel_id=1, source_target_pairs={{2,0},{4,2},{6,4},{3,1},{5,3},{7,5},{10,8},{12,10},{14,12},{11,9},... | collective-permute-start | bytes 6536 | tf_op jit(solution)/shard_map/ppermute | solution.py:15
  172.4 20.3 %copy-start.2 = (f32[12]{0:T(128)S(1)}, f32[12]{0:T(128)}, u32[]{:S(2)}) copy-start(f32[12]{0:T(128)} %param.11) | copy-start | bytes 148
  172.5 20.3 %copy-start.4 = (pred[8,17]{0,1:T(8,128)(4,1)S(1)}, pred[8,17]{0,1:T(8,128)(4,1)}, u32[]{:S(2)}) copy-start(pred[8,17]{0,1:T(8,128)(4,1)} %constant.49) | copy-start | bytes 412
  243.3 28.2 %copy-start.1 = (bf16[3,12]{1,0:T(4,128)(2,1)S(1)}, bf16[3,12]{1,0:T(4,128)(2,1)}, u32[]{:S(2)}) copy-start(bf16[3,12]{1,0:T(4,128)(2,1)} %param.12) | copy-start | bytes 220
  243.3 28.2 %copy-start.3 = (f32[3]{0:T(128)S(1)}, f32[3]{0:T(128)}, u32[]{:S(2)}) copy-start(f32[3]{0:T(128)} %param.13) | copy-start | bytes 40
where the time goes:
time: 274 us; the launch traced here: 273 us
  matrix products  113 us (41%)
  local copies, waits for them, and re-layouts  82.1 us (30%)
  blocking collectives  38.3 us (14%)
  waiting for transfers between devices  22.7 us (8%)
  starting transfers between devices  15.5 us (6%)
    conv_general_dilated x2, matrix products, convolve(): lax.conv_general_dilated(volume, kernel, (1, 1, 1), padding, dimension_nu...  113 us
    convert_element_type x3, local copies, waits for them, and re-layouts, activate(): jax.nn.relu(summed + bias[None, :, None, None, None]).astype(jnp.bfloat16)  39.4 us
    psum x1, blocking collectives, brick_normalize(): first_sum, second_sum = lax.psum((plain_sum, square_sum), ('sec', 'tile'))  38.3 us
    conv_general_dilated x4, local copies, waits for them, and re-layouts, convolve(): lax.conv_general_dilated(volume, kernel, (1, 1, 1), padding, dimension_nu...  28.8 us
    unnamed x16, local copies, waits for them, and re-layouts  10.6 us
    ppermute x2, waiting for transfers between devices, padded_2(): after = lax.ppermute(initial, axis, down)  10.3 us
    all_to_all x1, starting transfers between devices, regroup(): lax.all_to_all(volume, 'tile', split_axis=2, concat_axis=1, tiled=True)  6.32 us
    all_to_all x1, waiting for transfers between devices, regroup(): lax.all_to_all(volume, 'tile', split_axis=2, concat_axis=1, tiled=True)  6.07 us
  transfers between devices with their start and end apart: 6, of which 5 were waited for; matrix products, arithmetic and copies ran while one was open for 0% of the time, Pallas kernels for 0%

commit v1 on v0

v1 whole, which is shorter than its diff:
```python
import functools

import jax
import jax.numpy as jnp
import numpy as np
from jax import lax
from jax.experimental import pallas as pl
from jax.experimental.pallas import tpu as pltpu
from jax.sharding import PartitionSpec as P

LANES = 128
WIDE = 256
HALO_ROWS = 16
BF = jnp.bfloat16
F32 = jnp.float32


def exchange_kernel(
    secs, tiles, blocks, rows, x_ref, main, top, bottom, stats, stage, partial,
    send_m, recv_m, send_t, recv_t, send_b, recv_b, send_s, recv_s,
):
    s, t = lax.axis_index("sec"), lax.axis_index("tile")
    held = x_ref.shape[0]
    cols = x_ref.shape[2]
    staged = stage.shape[1]
    peers = secs * tiles
    home, place = t // blocks, t % blocks
    barrier = pltpu.get_barrier_semaphore()

    def greet(i, carry):
        s2, t2 = i // tiles, i % tiles

        @pl.when(jnp.logical_or(s2 != s, t2 != t))
        def _():
            pl.semaphore_signal(barrier, inc=1, device_id={"sec": s2, "tile": t2},
                                device_id_type=pl.DeviceIdType.MESH)

        return carry

    lax.fori_loop(0, peers, greet, 0)

    @pl.when(s == 0)
    def _():
        top[...] = jnp.zeros_like(top)

    @pl.when(s == secs - 1)
    def _():
        bottom[...] = jnp.zeros_like(bottom)

    sums = []
    squares = []
    for i in range(held):
        values = x_ref[i].astype(F32)
        moved = pltpu.roll(values, 2, 1)
        moved = jnp.concatenate([moved, moved[:, :LANES]], axis=1)
        if staged > rows:
            moved = jnp.concatenate(
                [moved, jnp.zeros((staged - rows, cols + LANES), F32)], axis=0)
        stage[i] = moved.astype(BF)
        col_sum = jnp.sum(values, axis=0, keepdims=True)
        col_square = jnp.sum(values * values, axis=0, keepdims=True)
        sums.append(sum(col_sum[:, c:c + LANES] for c in range(0, cols, LANES)))
        squares.append(sum(col_square[:, c:c + LANES] for c in range(0, cols, LANES)))
    packed = jnp.concatenate(
        sums + squares + [jnp.zeros((8 - 2 * held, LANES), F32)], axis=0)
    partial[...] = packed

    def remote(src, dst, send, recv, s2, t2):
        return pltpu.make_async_remote_copy(
            src_ref=src, dst_ref=dst, send_sem=send, recv_sem=recv,
            device_id={"sec": s2, "tile": t2}, device_id_type=pl.DeviceIdType.MESH)

    def begin(wanted, src, dst, send, recv, s2, t2):
        own = jnp.logical_and(s2 == s, t2 == t)

        @pl.when(jnp.logical_and(wanted, jnp.logical_not(own)))
        def _():
            remote(src, dst, send, recv, s2, t2).start()

        @pl.when(jnp.logical_and(wanted, own))
        def _():
            pltpu.make_async_copy(src, dst, recv).start()

    def sent(wanted, src, dst, send, recv, s2, t2):
        own = jnp.logical_and(s2 == s, t2 == t)

        @pl.when(jnp.logical_and(wanted, jnp.logical_not(own)))
        def _():
            remote(src, dst, send, recv, s2, t2).wait_send()

    def arrived(wanted, src, dst, send, recv, s2, t2):
        own = jnp.logical_and(s2 == s, t2 == t)

        @pl.when(jnp.logical_and(wanted, jnp.logical_not(own)))
        def _():
            remote(src, dst, send, recv, s2, t2).wait_recv()

        @pl.when(jnp.logical_and(wanted, own))
        def _():
            pltpu.make_async_copy(src, dst, recv).wait()

    pl.semaphore_wait(barrier, peers - 1)
    mine = pl.ds(s * held, held)
    goes_up = jnp.logical_and(place == 0, home > 0)
    goes_down = jnp.logical_and(place == blocks - 1, home < secs - 1)

    def out_stats(act):
        def body(i, carry):
            s2, t2 = i // tiles, i % tiles
            act(s2 >= 0, partial, stats.at[t, s], send_s.at[i], recv_s.at[s, t], s2, t2)
            return carry

        lax.fori_loop(0, peers, body, 0)

    def out_pixels(act):
        def body(t2, carry):
            window = pl.ds(pl.multiple_of(t2 * LANES, LANES), WIDE)
            act(t2 >= 0, stage.at[:, :, window], main.at[place, mine],
                send_m.at[t2], recv_m.at[s, place], home, t2)
            act(goes_up, stage.at[:, pl.ds(0, HALO_ROWS), window], bottom.at[mine],
                send_b.at[t2], recv_b.at[s], home - 1, t2)
            act(goes_down, stage.at[:, pl.ds(staged - HALO_ROWS, HALO_ROWS), window],
                top.at[mine], send_t.at[t2], recv_t.at[s], home + 1, t2)
            return carry

        lax.fori_loop(0, tiles, body, 0)

    out_pixels(begin)
    out_stats(begin)

    def in_pixels(s2, carry):
        window = pl.ds(pl.multiple_of(t * LANES, LANES), WIDE)
        theirs = pl.ds(s2 * held, held)

        def block(k, inner):
            arrived(s2 >= 0, stage.at[:, :, window], main.at[k, theirs],
                    send_m.at[0], recv_m.at[s2, k], s2, s * blocks + k)
            return inner

        lax.fori_loop(0, blocks, block, 0)
        arrived(s > 0, stage.at[:, pl.ds(staged - HALO_ROWS, HALO_ROWS), window],
                top.at[theirs], send_t.at[0], recv_t.at[s2], s2, s * blocks - 1)
        arrived(s < secs - 1, stage.at[:, pl.ds(0, HALO_ROWS), window], bottom.at[theirs],
                send_b.at[0], recv_b.at[s2], s2, (s + 1) * blocks)
        return carry

    lax.fori_loop(0, secs, in_pixels, 0)

    def in_stats(i, carry):
        s2, t2 = i // tiles, i % tiles
        arrived(s2 >= 0, partial, stats.at[t2, s2], send_s.at[0], recv_s.at[s2, t2], s2, t2)
        return carry

    lax.fori_loop(0, peers, in_stats, 0)
    out_pixels(sent)
    out_stats(sent)


def exchange(x, secs, tiles):
    held, rows, cols = x.shape
    brick_rows = rows * tiles // secs
    blocks = brick_rows // rows
    staged = max(rows, HALO_ROWS)
    sections = held * secs
    dma = pltpu.SemaphoreType.DMA
    vmem = pl.BlockSpec(memory_space=pltpu.VMEM)
    return pl.pallas_call(
        functools.partial(exchange_kernel, secs, tiles, blocks, rows),
        out_shape=[
            jax.ShapeDtypeStruct((blocks, sections, staged, WIDE), BF),
            jax.ShapeDtypeStruct((sections, HALO_ROWS, WIDE), BF),
            jax.ShapeDtypeStruct((sections, HALO_ROWS, WIDE), BF),
            jax.ShapeDtypeStruct((tiles, secs, 8, LANES), F32),
        ],
        in_specs=[vmem],
        out_specs=[vmem] * 4,
        scratch_shapes=[
            pltpu.VMEM((held, staged, cols + LANES), BF),
            pltpu.VMEM((8, LANES), F32),
            dma((tiles,)), dma((secs, blocks)),
            dma((tiles,)), dma((secs,)),
            dma((tiles,)), dma((secs,)),
            dma((secs * tiles,)), dma((secs, tiles)),
        ],
        compiler_params=pltpu.CompilerParams(
            collective_id=0, has_side_effects=True, vmem_limit_bytes=24 * 2**20),
        name="exchange",
    )(x)


SLOTS = 6
OUTSIDE = -1e30


def tables(zs, ch, aff):
    oz = ch * zs
    o_of = np.arange(oz) // zs
    z_of = np.arange(oz) % zs
    perm = np.zeros((zs * 16, zs * 16), np.float32)
    for y in range(16):
        for z in range(zs):
            perm[y * zs + z, z * 16 + y] = 1
    rows_pick = (o_of[:, None] == np.arange(ch)[None]).astype(np.float32)
    pick1 = np.tile(rows_pick, (3, 1))
    e1 = np.arange(3 * oz) // oz
    z1 = np.tile(z_of, 3)
    col = np.arange(3 * SLOTS * zs)
    b_col, slot, z_col = col // (SLOTS * zs), col // zs % SLOTS, col % zs
    place1 = (np.arange(3)[:, None] == b_col[None]).astype(np.float32)
    mask1 = np.zeros((9, 3 * oz, col.size), np.float32)
    for a in range(3):
        for e in range(3):
            mask1[a * 3 + e] = (
                (z_col[None] - z1[:, None] + 1 == a)
                & (slot[None] - e1[:, None] == e) & (slot[None] < 5))
    aux = (b_col == 1) & (slot == 5)
    bias_at = np.stack([(aux & (z_col == i)) for i in range(3)]).astype(np.float32)
    outside1 = np.where(
        aux[None] & (z_col[None] == 3 + e1[:, None]), OUTSIDE, 0.0).astype(np.float32)
    col2 = np.arange(3 * oz)
    ec = col2 // zs
    place2 = (np.arange(3 * ch)[:, None] == ec[None]).astype(np.float32)
    mask2 = np.stack(
        [(col2 % zs)[None] - z_of[:, None] + 1 == a for a in range(3)]).astype(np.float32)
    row = np.arange(aff * zs * 8)
    pick_h = ((row // (zs * 8))[:, None] == np.arange(aff)[None]).astype(np.float32)
    col_h = np.arange(8 * oz)
    place_h = (np.arange(ch)[:, None] == (col_h // zs % ch)[None]).astype(np.float32)
    mask_h = (
        ((row // 8 % zs)[:, None] == (col_h % zs)[None])
        & ((row % 8)[:, None] == (col_h // oz)[None])).astype(np.float32)
    as_bf = lambda v: jnp.asarray(v.astype(jnp.bfloat16))
    return [as_bf(v) for v in (
        perm, rows_pick, pick1, place1, mask1, bias_at[:, None, :], outside1, place2, mask2,
        pick_h, place_h, mask_h)]


def dot(a, b):
    return jnp.dot(a, b, preferred_element_type=F32)


def compute_kernel(
    secs, tiles, rows, cells, main, top, bottom, stats, k1, k2, kh, b1, b2, bh,
    perm, pick2, pick1, place1, mask1, bias_at, outside1, place2, mask2, pick_h, place_h, mask_h,
    out, w1, w2, wh, bias2, bias_h, shifted, first,
):
    s, t = lax.axis_index("sec"), lax.axis_index("tile")
    aff, zs, brick_rows, brick_cols = out.shape
    blocks, _, staged, _ = main.shape
    held = zs // secs
    ch = b1.shape[0]
    oz = ch * zs

    bias1 = jnp.concatenate(
        [jnp.full((zs, w1.shape[1]), b1[o], F32) for _ in range(3) for o in range(ch)], axis=0)
    high = bias1.astype(BF).astype(F32)
    mid = (bias1 - high).astype(BF).astype(F32)
    low = bias1 - high - mid
    built = outside1[...].astype(F32)
    for i, part in enumerate((high, mid, low)):
        built = built + part * bias_at[i].astype(F32)
    for i in range(9):
        placed = dot(dot(pick1[...], k1[i]).astype(BF), place1[...])
        built = built + placed * mask1[i].astype(F32)
    w1[...] = built.astype(BF)
    blocks_row = [[jnp.zeros((oz, 3 * oz), BF)] * 4 for _ in range(2)]
    for b in range(3):
        band = jnp.zeros((oz, 3 * oz), F32)
        for a in range(3):
            placed = dot(dot(pick2[...], k2[a * 3 + b]).astype(BF), place2[...])
            band = band + placed * mask2[a].astype(F32)
        band = band.astype(BF)
        for p in range(2):
            blocks_row[p][b + p] = band
    w2[...] = jnp.concatenate(
        [jnp.concatenate(blocks_row[p], axis=1) for p in range(2)], axis=0)
    wh[...] = (dot(dot(pick_h[...], kh[...]).astype(BF), place_h[...])
               * mask_h[...].astype(F32)).astype(BF)
    bias2[...] = jnp.concatenate(
        [jnp.full((zs, WIDE), b2[o], F32) for _ in range(2) for o in range(ch)], axis=0)
    bias_h[...] = jnp.concatenate(
        [jnp.full((zs * 8, LANES), bh[k], F32) for k in range(aff)], axis=0)

    summed = jnp.sum(stats[...], axis=0)
    summed = jnp.sum(summed, axis=2, keepdims=True)
    total = jnp.concatenate([summed[i, 0:held] for i in range(secs)], axis=0)
    square = jnp.concatenate([summed[i, held:2 * held] for i in range(secs)], axis=0)
    average = total / cells
    variance = square / cells - average * average
    inv_std = jnp.broadcast_to(lax.rsqrt(variance + 1e-05), (zs, WIDE))
    average = jnp.broadcast_to(average, (zs, WIDE))

    lane = lax.broadcasted_iota(jnp.int32, (16, zs, WIDE), 2) - 2 + t * brick_cols
    col_inside = (lane >= 0) & (lane < brick_cols * tiles)
    slot = lax.broadcasted_iota(jnp.int32, (16, zs, LANES), 1)
    x_at = lax.broadcasted_iota(jnp.int32, (16, zs, LANES), 2) + t * brick_cols
    y_in = lax.broadcasted_iota(jnp.int32, (16, zs, LANES), 0)
    x_seen = x_at + slot - 4
    x_outside = (x_seen < 0) | (x_seen >= brick_cols * tiles)

    def spread(raw, row0, inside):
        turned = dot(perm[...], raw.reshape(zs * 16, WIDE)).reshape(16, zs, WIDE)
        normed = (turned - average[None]) * inv_std[None]
        normed = jnp.where(col_inside & inside, normed, 0.0).reshape(16 * zs, WIDE)
        parts = [normed[:, :LANES]]
        for i in range(1, 5):
            parts.append(pltpu.roll(normed, WIDE - i, 1)[:, :LANES])
        y_at = y_in + row0 + s * brick_rows
        y_outside = (y_at < 0) | (y_at >= brick_rows * secs)
        aux = jnp.where(
            slot < 3, 1.0, jnp.where((slot < 6) & (y_outside | x_outside), 1.0, 0.0))
        parts = [part.reshape(16, zs, LANES) for part in parts] + [aux]
        return jnp.concatenate(parts, axis=1).astype(BF)

    step = min(rows, 16)
    for k in range(blocks):
        for q in range(staged // 16):
            row0 = k * rows + q * 16
            ready = spread(main[k, :, q * 16:q * 16 + 16, :], row0, True)
            shifted[2 + row0:2 + row0 + step] = ready[:step]
    last = rows - 2 - (staged - HALO_ROWS)
    shifted[0:2] = spread(top[...], -2 - last, s > 0)[last:last + 2]
    shifted[2 + brick_rows:4 + brick_rows] = spread(bottom[...], brick_rows, s < secs - 1)[0:2]

    depth1 = w1.shape[1]

    def layer_one(i, carry):
        j = 2 * i
        x = jnp.concatenate(
            [shifted[pl.ds(j + d, 3)].reshape(depth1, LANES) for d in range(2)], axis=1)
        y = jnp.maximum(dot(w1[...], x), 0.0).astype(BF)
        first[j] = y[:, :LANES]
        first[j + 1] = y[:, LANES:]
        return carry

    lax.fori_loop(0, (brick_rows + 2) // 2, layer_one, 0, unroll=3)

    def layer_two(i, carry):
        found = []
        for h in range(2):
            j = 8 * i + 4 * h
            x = jnp.concatenate(
                [first[pl.ds(j + d, 4)].reshape(12 * oz, LANES) for d in (0, 2)], axis=1)
            y = jnp.maximum(dot(w2[...], x) + bias2[...], 0.0).astype(BF)
            found += [y[:, :LANES], y[:, LANES:]]
        logits = dot(wh[...], jnp.concatenate(found, axis=0)) + bias_h[...]
        out[:, :, pl.ds(pl.multiple_of(8 * i, 8), 8), :] = jax.nn.sigmoid(logits).reshape(
            aff, zs, 8, LANES)
        return carry

    lax.fori_loop(0, brick_rows // 8, layer_two, 0, unroll=2)


def compute(pixels, k1, b1, k2, b2, kh, bh, secs, tiles, rows):
    main = pixels[0]
    blocks, zs = main.shape[:2]
    brick_rows = blocks * rows
    ch, aff = b1.shape[0], bh.shape[0]
    oz = ch * zs
    cells = brick_rows * secs * LANES * tiles
    k1 = jnp.transpose(k1[:, 0], (1, 3, 0, 2)).reshape(9, ch, 3)
    k2 = jnp.transpose(k2, (2, 3, 0, 4, 1)).reshape(9, ch, 3 * ch)
    consts = tables(zs, ch, aff)
    vmem = pl.BlockSpec(memory_space=pltpu.VMEM)
    smem = pl.BlockSpec(memory_space=pltpu.SMEM)
    return pl.pallas_call(
        functools.partial(compute_kernel, secs, tiles, rows, cells),
        out_shape=jax.ShapeDtypeStruct((aff, zs, brick_rows, LANES), F32),
        in_specs=[vmem] * 7 + [smem] * 3 + [vmem] * len(consts),
        out_specs=vmem,
        scratch_shapes=[
            pltpu.VMEM((3 * oz, 3 * SLOTS * zs), BF),
            pltpu.VMEM((2 * oz, 12 * oz), BF),
            pltpu.VMEM((aff * zs * 8, 8 * oz), BF),
            pltpu.VMEM((2 * oz, WIDE), F32),
            pltpu.VMEM((aff * zs * 8, LANES), F32),
            pltpu.VMEM((brick_rows + 4, SLOTS * zs, LANES), BF),
            pltpu.VMEM((brick_rows + 2, 3 * oz, LANES), BF),
        ],
        compiler_params=pltpu.CompilerParams(vmem_limit_bytes=40 * 2**20),
        name="predict",
    )(*pixels, k1, k2, kh, b1, b2, bh, *consts)


def per_device(
    sections_in, first_kernel, first_bias, second_kernel, second_bias, head_kernel, head_bias
):
    secs, tiles = lax.axis_size("sec"), lax.axis_size("tile")
    pixels = exchange(sections_in, secs, tiles)
    return compute(
        pixels, first_kernel, first_bias, second_kernel, second_bias, head_kernel, head_bias,
        secs, tiles, sections_in.shape[1])


def solution(mesh):
    in_specs = (P("sec", "tile", "half"), P(), P(), P(), P(), P(), P())
    out_specs = P(None, None, "sec", ("half", "tile"))
    return jax.shard_map(
        per_device, mesh=mesh, in_specs=in_specs, out_specs=out_specs, check_vma=False
    )
```

time: 274 us -> 45.7 us (0.17)
  matrix products: 113 us -> 0 us
  local copies, waits for them, and re-layouts: 82.1 us -> 15.6 us
  blocking collectives: 38.3 us -> 0 us
  Pallas kernels: 0 us -> 29.3 us
  waiting for transfers between devices: 22.7 us -> 0 us
  starting transfers between devices: 15.5 us -> 0 us
    conv_general_dilated x2 -> x0, matrix products: 113 us -> none  [convolve(): lax.conv_general_dilated(volume, kernel, (1, 1, 1), padding, dimension_nu...]
    convert_element_type x4 -> x0, local copies, waits for them, and re-layouts: 39.4 us -> none  [the longest x3 39.4 us: activate(): jax.nn.relu(summed + bias[None, :, None, None, None]).astype(jnp.bfloat16)]
    psum x1 -> x0, blocking collectives: 38.3 us -> none  [brick_normalize(): first_sum, second_sum = lax.psum((plain_sum, square_sum), ('sec', 'tile'))]
    pallas_call x0 -> x2, Pallas kernels: none -> 29.3 us  [the longest x1 17.6 us: exchange(): pl.pallas_call(functools.partial(exchange_kernel, secs, tiles, blocks, ro...]
    conv_general_dilated x4 -> x0, local copies, waits for them, and re-layouts: 28.8 us -> none  [convolve(): lax.conv_general_dilated(volume, kernel, (1, 1, 1), padding, dimension_nu...]
    ppermute x4 -> x0, waiting for transfers between devices: 11.6 us -> none  [the longest x2 10.3 us: padded_2(): after = lax.ppermute(initial, axis, down)]
    all_to_all x2 -> x0, waiting for transfers between devices: 11.1 us -> none  [the longest x1 6.07 us: regroup(): lax.all_to_all(volume, 'tile', split_axis=2, concat_axis=1, tiled=True)]
    all_to_all x2 -> x0, starting transfers between devices: 10 us -> none  [the longest x1 6.32 us: regroup(): lax.all_to_all(volume, 'tile', split_axis=2, concat_axis=1, tiled=True)]
  transfers between devices with their start and end apart: 6 -> 0, of which waited for: 5 -> 0; matrix products, arithmetic and copies ran while one was open for 0% -> 0% of each run, Pallas kernels for 0% -> 0%
where the time goes in v1:
time: 45.7 us; the launch traced here: 44.9 us
  Pallas kernels  29.3 us (64%)
  local copies, waits for them, and re-layouts  15.6 us (34%)
    pallas_call x1, Pallas kernels, exchange(): pl.pallas_call(functools.partial(exchange_kernel, secs, tiles, blocks, ro...  17.6 us
    unnamed x34, local copies, waits for them, and re-layouts  13.7 us
    pallas_call x1, Pallas kernels, compute(): pl.pallas_call(functools.partial(compute_kernel, secs, tiles, rows, cells...  11.7 us
    reshape x2, local copies, waits for them, and re-layouts, compute(): k2 = jnp.transpose(k2, (2, 3, 0, 4, 1)).reshape(9, ch, 3 * ch)  1.04 us

profile of v1, /device:TPU:0, one launch (start us, length us, event | category | flops | bytes accessed | tf_op | source)
XLA Modules:
  0.0 44.9 jit_solution(14627793195690316686)
XLA Ops:
  0.0 0.8 %copy.20 = bf16[3,3,12,3]{3,2,1,0:T(8,128)(2,1)S(1)} copy(bf16[3,3,12,3]{2,1,3,0:T(4,128)(2,1)} %bitcast.9) | data formatting | bytes 1296 | tf_op jit(solution)/shard_map/transpose | solution.py:361
  0.8 1.0 %reshape.8 = bf16[9,12,36]{2,0,1:T(8,128)(2,1)S(1)} reshape(bf16[3,3,12,3,12]{4,3,1,0,2:T(4,128)(2,1)} %bitcast.8) | data formatting | bytes 15552 | tf_op jit(solution)/shard_map/reshape | solution.py:362
  1.9 0.0 copy-start.4
  1.9 0.9 %copy-done.4 = bf16[2,64,512]{2,1,0:T(8,128)(2,1)S(1)} copy-done((bf16[2,64,512]{2,1,0:T(8,128)(2,1)S(1)}, bf16[2,64,512]{2,1,0:T(8,128)(2,1)}, u32[]{:S(2)}) %copy-start.4) | copy-done | bytes 131096
  2.8 17.6 %exchange.1 = (bf16[1,8,64,256]{3,2,1,0:T(8,128)(2,1)S(1)}, bf16[8,16,256]{2,1,0:T(8,128)(2,1)S(1)}, bf16[8,16,256]{2,1,0:T(8,128)(2,1)S(1)}, f32[4,4,8,128]{3,2,1,0:T(8,128)S(1)}) custom-call(bf16[2,64,512]{2,1,0:T(8,128)(2,1)S(1)} %copy-done.4), custom_call_target="tpu_custom_call" | custom-call | tf_op jit(solution)/shard_map/exchange/pallas_call | solution.py:167
  20.4 0.0 copy-start
  20.4 1.3 %copy-done = bf16[9,288,144]{2,1,0:T(8,128)(2,1)S(1)} copy-done((bf16[9,288,144]{2,1,0:T(8,128)(2,1)S(1)}, bf16[9,288,144]{2,1,0:T(8,128)(2,1)}, u32[]{:S(2)}) %copy-start) | copy-done | bytes 746520
  21.7 0.0 copy-start.1
  21.7 1.0 %copy-done.1 = bf16[192,768]{1,0:T(8,128)(2,1)S(1)} copy-done((bf16[192,768]{1,0:T(8,128)(2,1)S(1)}, bf16[192,768]{1,0:T(8,128)(2,1)}, u32[]{:S(2)}) %copy-start.1) | copy-done | bytes 294936
  22.7 0.0 copy-start.2
  22.7 0.9 %copy-done.2 = bf16[3,96,288]{2,1,0:T(8,128)(2,1)S(1)} copy-done((bf16[3,96,288]{2,1,0:T(8,128)(2,1)S(1)}, bf16[3,96,288]{2,1,0:T(8,128)(2,1)}, u32[]{:S(2)}) %copy-start.2) | copy-done | bytes 165912
  23.6 0.0 copy-start.3
  23.6 0.9 %copy-done.3 = bf16[288,144]{1,0:T(8,128)(2,1)S(1)} copy-done((bf16[288,144]{1,0:T(8,128)(2,1)S(1)}, bf16[288,144]{1,0:T(8,128)(2,1)}, u32[]{:S(2)}) %copy-start.3) | copy-done | bytes 82968
  24.5 0.0 copy-start.5
  24.5 0.9 %copy-done.5 = bf16[288,12]{1,0:T(8,128)(2,1)S(1)} copy-done((bf16[288,12]{1,0:T(8,128)(2,1)S(1)}, bf16[288,12]{1,0:T(8,128)(2,1)}, u32[]{:S(2)}) %copy-start.5) | copy-done | bytes 6936
  25.4 0.0 copy-start.6
  25.4 0.8 %copy-done.6 = bf16[192,3]{1,0:T(8,128)(2,1)S(1)} copy-done((bf16[192,3]{1,0:T(8,128)(2,1)S(1)}, bf16[192,3]{1,0:T(8,128)(2,1)}, u32[]{:S(2)}) %copy-start.6) | copy-done | bytes 1176
  26.2 0.0 copy-start.7
  26.2 0.8 %copy-done.7 = bf16[128,128]{1,0:T(8,128)(2,1)S(1)} copy-done((bf16[128,128]{1,0:T(8,128)(2,1)S(1)}, bf16[128,128]{1,0:T(8,128)(2,1)}, u32[]{:S(2)}) %copy-start.7) | copy-done | bytes 32792
  27.0 0.0 copy-start.8
  27.0 0.8 %copy-done.8 = bf16[36,288]{1,0:T(8,128)(2,1)S(1)} copy-done((bf16[36,288]{1,0:T(8,128)(2,1)S(1)}, bf16[36,288]{1,0:T(8,128)(2,1)}, u32[]{:S(2)}) %copy-start.8) | copy-done | bytes 20760
  27.7 0.0 copy-start.9
  27.7 0.7 %copy-done.9 = bf16[12,768]{1,0:T(8,128)(2,1)S(1)} copy-done((bf16[12,768]{1,0:T(8,128)(2,1)S(1)}, bf16[12,768]{1,0:T(8,128)(2,1)}, u32[]{:S(2)}) %copy-start.9) | copy-done | bytes 18456
  28.5 0.0 copy-start.10
  28.5 0.7 %copy-done.10 = bf16[96,12]{1,0:T(8,128)(2,1)S(1)} copy-done((bf16[96,12]{1,0:T(8,128)(2,1)S(1)}, bf16[96,12]{1,0:T(8,128)(2,1)}, u32[]{:S(2)}) %copy-start.10) | copy-done | bytes 2328
  29.2 0.0 copy-start.11
  29.2 0.7 %copy-done.11 = bf16[3,1,144]{2,1,0:T(2,128)(2,1)S(1)} copy-done((bf16[3,1,144]{2,1,0:T(2,128)(2,1)S(1)}, bf16[3,1,144]{2,1,0:T(2,128)(2,1)}, u32[]{:S(2)}) %copy-start.11) | copy-done | bytes 888
  29.9 0.0 copy-start.12
  29.9 0.7 %copy-done.12 = bf16[3,144]{1,0:T(4,128)(2,1)S(1)} copy-done((bf16[3,144]{1,0:T(4,128)(2,1)S(1)}, bf16[3,144]{1,0:T(4,128)(2,1)}, u32[]{:S(2)}) %copy-start.12) | copy-done | bytes 888
  30.6 0.0 copy-start.13
  30.6 0.7 %copy-done.13 = bf16[3,12]{1,0:T(4,128)(2,1)S(1)} copy-done((bf16[3,12]{1,0:T(4,128)(2,1)S(1)}, bf16[3,12]{1,0:T(4,128)(2,1)}, u32[]{:S(2)}) %copy-start.13) | copy-done | bytes 96
  31.2 0.0 copy-start.14
  31.3 0.7 %copy-done.14 = f32[12]{0:T(128)S(1)} copy-done((f32[12]{0:T(128)S(1)}, f32[12]{0:T(128)}, u32[]{:S(2)}) %copy-start.14) | copy-done | bytes 72
  31.9 0.0 copy-start.15
  31.9 0.7 %copy-done.15 = f32[12]{0:T(128)S(1)} copy-done((f32[12]{0:T(128)S(1)}, f32[12]{0:T(128)}, u32[]{:S(2)}) %copy-start.15) | copy-done | bytes 72
  32.6 0.0 copy-start.16
  32.6 0.7 %copy-done.16 = f32[3]{0:T(128)S(1)} copy-done((f32[3]{0:T(128)S(1)}, f32[3]{0:T(128)}, u32[]{:S(2)}) %copy-start.16) | copy-done | bytes 36
  33.2 11.7 %predict.1 = f32[3,8,64,128]{3,2,1,0:T(8,128)} custom-call(bf16[1,8,64,256]{3,2,1,0:T(8,128)(2,1)S(1)} %get-tuple-element.9.main, bf16[8,16,256]{2,1,0:T(8,128)(2,1)S(1)} %get-tuple-element.10.top, bf16[8,16,256]{2,1,0:T(8,128)(2,1)S(1)} %get-tuple-element.11.bottom, f32[4,4,8,128]{3,2,1,0:T(8,128)S(1)} %get-tuple-element.12.stats, ...), custom_call_target="tpu_custom_call" | custom-call | tf_op jit(solution)/shard_map/predict/pallas_call | solution.py:366
  (1 shorter events, 0.0 us)
Async XLA Ops:
  1.9 0.9 %copy-start.4 = (bf16[2,64,512]{2,1,0:T(8,128)(2,1)S(1)}, bf16[2,64,512]{2,1,0:T(8,128)(2,1)}, u32[]{:S(2)}) copy-start(bf16[2,64,512]{2,1,0:T(8,128)(2,1)} %x_ref.1) | copy-start | bytes 393220
  20.4 1.3 %copy-start = (bf16[9,288,144]{2,1,0:T(8,128)(2,1)S(1)}, bf16[9,288,144]{2,1,0:T(8,128)(2,1)}, u32[]{:S(2)}) copy-start(bf16[9,288,144]{2,1,0:T(8,128)(2,1)} %constant.28.clone.mask1) | copy-start | bytes 2239492
  21.7 1.0 %copy-start.1 = (bf16[192,768]{1,0:T(8,128)(2,1)S(1)}, bf16[192,768]{1,0:T(8,128)(2,1)}, u32[]{:S(2)}) copy-start(bf16[192,768]{1,0:T(8,128)(2,1)} %constant.35.clone.mask_h) | copy-start | bytes 884740
  22.7 0.9 %copy-start.2 = (bf16[3,96,288]{2,1,0:T(8,128)(2,1)S(1)}, bf16[3,96,288]{2,1,0:T(8,128)(2,1)}, u32[]{:S(2)}) copy-start(bf16[3,96,288]{2,1,0:T(8,128)(2,1)} %constant.32.clone.mask2) | copy-start | bytes 497668
  23.6 0.9 %copy-start.3 = (bf16[288,144]{1,0:T(8,128)(2,1)S(1)}, bf16[288,144]{1,0:T(8,128)(2,1)}, u32[]{:S(2)}) copy-start(bf16[288,144]{1,0:T(8,128)(2,1)} %constant.30.clone.outside1) | copy-start | bytes 248836
  24.5 0.9 %copy-start.5 = (bf16[288,12]{1,0:T(8,128)(2,1)S(1)}, bf16[288,12]{1,0:T(8,128)(2,1)}, u32[]{:S(2)}) copy-start(bf16[288,12]{1,0:T(8,128)(2,1)} %constant.26.clone.pick1) | copy-start | bytes 20740
  25.4 0.8 %copy-start.6 = (bf16[192,3]{1,0:T(8,128)(2,1)S(1)}, bf16[192,3]{1,0:T(8,128)(2,1)}, u32[]{:S(2)}) copy-start(bf16[192,3]{1,0:T(8,128)(2,1)} %constant.33.clone.pick_h) | copy-start | bytes 3460
  26.2 0.8 %copy-start.7 = (bf16[128,128]{1,0:T(8,128)(2,1)S(1)}, bf16[128,128]{1,0:T(8,128)(2,1)}, u32[]{:S(2)}) copy-start(bf16[128,128]{1,0:T(8,128)(2,1)} %constant.24.clone.perm) | copy-start | bytes 98308
  27.0 0.8 %copy-start.8 = (bf16[36,288]{1,0:T(8,128)(2,1)S(1)}, bf16[36,288]{1,0:T(8,128)(2,1)}, u32[]{:S(2)}) copy-start(bf16[36,288]{1,0:T(8,128)(2,1)} %constant.31.clone.place2) | copy-start | bytes 62212
  27.7 0.7 %copy-start.9 = (bf16[12,768]{1,0:T(8,128)(2,1)S(1)}, bf16[12,768]{1,0:T(8,128)(2,1)}, u32[]{:S(2)}) copy-start(bf16[12,768]{1,0:T(8,128)(2,1)} %constant.34.clone.place_h) | copy-start | bytes 55300
  28.5 0.7 %copy-start.10 = (bf16[96,12]{1,0:T(8,128)(2,1)S(1)}, bf16[96,12]{1,0:T(8,128)(2,1)}, u32[]{:S(2)}) copy-start(bf16[96,12]{1,0:T(8,128)(2,1)} %constant.25.clone.pick2) | copy-start | bytes 6916
  29.2 0.7 %copy-start.11 = (bf16[3,1,144]{2,1,0:T(2,128)(2,1)S(1)}, bf16[3,1,144]{2,1,0:T(2,128)(2,1)}, u32[]{:S(2)}) copy-start(bf16[3,1,144]{2,1,0:T(2,128)(2,1)} %constant.29.clone.bias_at) | copy-start | bytes 2596
  29.9 0.7 %copy-start.12 = (bf16[3,144]{1,0:T(4,128)(2,1)S(1)}, bf16[3,144]{1,0:T(4,128)(2,1)}, u32[]{:S(2)}) copy-start(bf16[3,144]{1,0:T(4,128)(2,1)} %constant.27.clone.place1) | copy-start | bytes 2596
  30.6 0.7 %copy-start.13 = (bf16[3,12]{1,0:T(4,128)(2,1)S(1)}, bf16[3,12]{1,0:T(4,128)(2,1)}, u32[]{:S(2)}) copy-start(bf16[3,12]{1,0:T(4,128)(2,1)} %kh.1) | copy-start | bytes 220
  31.2 0.7 %copy-start.14 = (f32[12]{0:T(128)S(1)}, f32[12]{0:T(128)}, u32[]{:S(2)}) copy-start(f32[12]{0:T(128)} %b1.1) | copy-start | bytes 148
  31.9 0.7 %copy-start.15 = (f32[12]{0:T(128)S(1)}, f32[12]{0:T(128)}, u32[]{:S(2)}) copy-start(f32[12]{0:T(128)} %b2.1) | copy-start | bytes 148
  32.6 0.7 %copy-start.16 = (f32[3]{0:T(128)S(1)}, f32[3]{0:T(128)}, u32[]{:S(2)}) copy-start(f32[3]{0:T(128)} %bh.1) | copy-start | bytes 40

commit v2 on v1

--- a/solution.py
+++ b/solution.py
@@ -15,10 +15,59 @@
 F32 = jnp.float32
 
 
+def dot(a, b):
+    return jnp.dot(a, b, preferred_element_type=F32)
+
+
+def build_weights(
+    zs, k1, k2, kh, b1, b2, bh, pick2, pick1, place1, mask1, bias_at, outside1,
+    place2, mask2, pick_h, place_h, mask_h, w1, w2, wh, bias2, bias_h,
+):
+    ch, aff = b1.shape[0], bh.shape[0]
+    oz = ch * zs
+    bias1 = jnp.concatenate(
+        [jnp.full((zs, w1.shape[1]), b1[o], F32) for _ in range(3) for o in range(ch)], axis=0)
+    high = bias1.astype(BF).astype(F32)
+    mid = (bias1 - high).astype(BF).astype(F32)
+    low = bias1 - high - mid
+    built = outside1[...].astype(F32)
+    for i, part in enumerate((high, mid, low)):
+        built = built + part * bias_at[i].astype(F32)
+    for i in range(9):
+        placed = dot(dot(pick1[...], k1[i]).astype(BF), place1[...])
+        built = built + placed * mask1[i].astype(F32)
+    w1[...] = built.astype(BF)
+    blocks_row = [[jnp.zeros((oz, 3 * oz), BF)] * 4 for _ in range(2)]
+    for b in range(3):
+        band = jnp.zeros((oz, 3 * oz), F32)
+        for a in range(3):
+            placed = dot(dot(pick2[...], k2[a * 3 + b]).astype(BF), place2[...])
+            band = band + placed * mask2[a].astype(F32)
+        band = band.astype(BF)
+        for p in range(2):
+            blocks_row[p][b + p] = band
+    w2[...] = jnp.concatenate(
+        [jnp.concatenate(blocks_row[p], axis=1) for p in range(2)], axis=0)
+    wh[...] = (dot(dot(pick_h[...], kh[...]).astype(BF), place_h[...])
+               * mask_h[...].astype(F32)).astype(BF)
+    bias2[...] = jnp.concatenate(
+        [jnp.full((zs, WIDE), b2[o], F32) for _ in range(2) for o in range(ch)], axis=0)
+    bias_h[...] = jnp.concatenate(
+        [jnp.full((zs * 8, LANES), bh[k], F32) for k in range(aff)], axis=0)
+
+
 def exchange_kernel(
-    secs, tiles, blocks, rows, x_ref, main, top, bottom, stats, stage, partial,
-    send_m, recv_m, send_t, recv_t, send_b, recv_b, send_s, recv_s,
+    secs, tiles, blocks, rows, count, *refs,
 ):
+    far = refs[:count]
+    out = refs[count]
+    arrivals = refs[count + 1:count + 11]
+    main, top, bottom, stats, w1, w2, wh, bias2, bias_h, perm = arrivals
+    near = refs[count + 11:2 * count + 10] + (perm,)
+    shifted, first, load, stage, partial = refs[2 * count + 10:2 * count + 15]
+    (send_m, recv_m, send_t, recv_t, send_b, recv_b, send_s, recv_s) = refs[2 * count + 15:]
+    loads = [pltpu.make_async_copy(far[i], near[i], load.at[i]) for i in range(count)]
+    x_ref = near[0]
     s, t = lax.axis_index("sec"), lax.axis_index("tile")
     held = x_ref.shape[0]
     cols = x_ref.shape[2]
@@ -37,6 +86,8 @@
 
         return carry
 
+    for copy in loads:
+        copy.start()
     lax.fori_loop(0, peers, greet, 0)
 
     @pl.when(s == 0)
@@ -47,6 +98,7 @@
     def _():
         bottom[...] = jnp.zeros_like(bottom)
 
+    loads[0].wait()
     sums = []
     squares = []
     for i in range(held):
@@ -127,6 +179,9 @@
 
     out_pixels(begin)
     out_stats(begin)
+    for copy in loads[1:]:
+        copy.wait()
+    build_weights(main.shape[1], *near[1:-1], w1, w2, wh, bias2, bias_h)
 
     def in_pixels(s2, carry):
         window = pl.ds(pl.multiple_of(t * LANES, LANES), WIDE)
@@ -152,40 +207,10 @@
         return carry
 
     lax.fori_loop(0, peers, in_stats, 0)
+    cells = rows * tiles * cols
+    compute_kernel(secs, tiles, rows, cells, *arrivals, out, shifted, first)
     out_pixels(sent)
     out_stats(sent)
-
-
-def exchange(x, secs, tiles):
-    held, rows, cols = x.shape
-    brick_rows = rows * tiles // secs
-    blocks = brick_rows // rows
-    staged = max(rows, HALO_ROWS)
-    sections = held * secs
-    dma = pltpu.SemaphoreType.DMA
-    vmem = pl.BlockSpec(memory_space=pltpu.VMEM)
-    return pl.pallas_call(
-        functools.partial(exchange_kernel, secs, tiles, blocks, rows),
-        out_shape=[
-            jax.ShapeDtypeStruct((blocks, sections, staged, WIDE), BF),
-            jax.ShapeDtypeStruct((sections, HALO_ROWS, WIDE), BF),
-            jax.ShapeDtypeStruct((sections, HALO_ROWS, WIDE), BF),
-            jax.ShapeDtypeStruct((tiles, secs, 8, LANES), F32),
-        ],
-        in_specs=[vmem],
-        out_specs=[vmem] * 4,
-        scratch_shapes=[
-            pltpu.VMEM((held, staged, cols + LANES), BF),
-            pltpu.VMEM((8, LANES), F32),
-            dma((tiles,)), dma((secs, blocks)),
-            dma((tiles,)), dma((secs,)),
-            dma((tiles,)), dma((secs,)),
-            dma((secs * tiles,)), dma((secs, tiles)),
-        ],
-        compiler_params=pltpu.CompilerParams(
-            collective_id=0, has_side_effects=True, vmem_limit_bytes=24 * 2**20),
-        name="exchange",
-    )(x)
 
 
 SLOTS = 6
@@ -235,51 +260,65 @@
         pick_h, place_h, mask_h)]
 
 
-def dot(a, b):
-    return jnp.dot(a, b, preferred_element_type=F32)
+def exchange(x, k1, b1, k2, b2, kh, bh, secs, tiles):
+    held, rows, cols = x.shape
+    brick_rows = rows * tiles // secs
+    blocks = brick_rows // rows
+    staged = max(rows, HALO_ROWS)
+    zs = held * secs
+    ch, aff = b1.shape[0], bh.shape[0]
+    oz = ch * zs
+    k1 = jnp.transpose(k1[:, 0], (1, 3, 0, 2)).reshape(9, ch, 3)
+    k2 = jnp.transpose(k2, (2, 3, 0, 4, 1)).reshape(9, ch, 3 * ch)
+    perm, *consts = tables(zs, ch, aff)
+    operands = [x, k1, k2, kh, b1, b2, bh, *consts, perm]
+    dma = pltpu.SemaphoreType.DMA
+    vmem = pl.BlockSpec(memory_space=pltpu.VMEM)
+    hbm = pl.BlockSpec(memory_space=pltpu.HBM)
+    near = [
+        (pltpu.SMEM if v.ndim == 1 else pltpu.VMEM)(v.shape, v.dtype) for v in operands[:-1]]
+    return pl.pallas_call(
+        functools.partial(exchange_kernel, secs, tiles, blocks, rows, len(operands)),
+        out_shape=jax.ShapeDtypeStruct((aff, zs, brick_rows, LANES), F32),
+        in_specs=[hbm] * len(operands),
+        out_specs=vmem,
+        scratch_shapes=[
+            pltpu.VMEM((blocks, zs, staged, WIDE), BF),
+            pltpu.VMEM((zs, HALO_ROWS, WIDE), BF),
+            pltpu.VMEM((zs, HALO_ROWS, WIDE), BF),
+            pltpu.VMEM((tiles, secs, 8, LANES), F32),
+            pltpu.VMEM((3 * oz, 3 * SLOTS * zs), BF),
+            pltpu.VMEM((2 * oz, 12 * oz), BF),
+            pltpu.VMEM((aff * zs * 8, 8 * oz), BF),
+            pltpu.VMEM((2 * oz, WIDE), F32),
+            pltpu.VMEM((aff * zs * 8, LANES), F32),
+            pltpu.VMEM(perm.shape, BF),
+        ] + near + [
+            pltpu.VMEM((brick_rows + 4, SLOTS * zs, LANES), BF),
+            pltpu.VMEM((brick_rows + 2, 3 * oz, LANES), BF),
+            dma((len(operands),)),
+            pltpu.VMEM((held, staged, cols + LANES), BF),
+            pltpu.VMEM((8, LANES), F32),
+            dma((tiles,)), dma((secs, blocks)),
+            dma((tiles,)), dma((secs,)),
+            dma((tiles,)), dma((secs,)),
+            dma((secs * tiles,)), dma((secs, tiles)),
+        ],
+        compiler_params=pltpu.CompilerParams(
+            collective_id=0, has_side_effects=True, vmem_limit_bytes=60 * 2**20),
+        name="predict",
+    )(*operands)
 
 
 def compute_kernel(
-    secs, tiles, rows, cells, main, top, bottom, stats, k1, k2, kh, b1, b2, bh,
-    perm, pick2, pick1, place1, mask1, bias_at, outside1, place2, mask2, pick_h, place_h, mask_h,
-    out, w1, w2, wh, bias2, bias_h, shifted, first,
+    secs, tiles, rows, cells, main, top, bottom, stats, w1, w2, wh, bias2, bias_h, perm,
+    out, shifted, first,
 ):
     s, t = lax.axis_index("sec"), lax.axis_index("tile")
     aff, zs, brick_rows, brick_cols = out.shape
     blocks, _, staged, _ = main.shape
     held = zs // secs
-    ch = b1.shape[0]
-    oz = ch * zs
-
-    bias1 = jnp.concatenate(
-        [jnp.full((zs, w1.shape[1]), b1[o], F32) for _ in range(3) for o in range(ch)], axis=0)
-    high = bias1.astype(BF).astype(F32)
-    mid = (bias1 - high).astype(BF).astype(F32)
-    low = bias1 - high - mid
-    built = outside1[...].astype(F32)
-    for i, part in enumerate((high, mid, low)):
-        built = built + part * bias_at[i].astype(F32)
-    for i in range(9):
-        placed = dot(dot(pick1[...], k1[i]).astype(BF), place1[...])
-        built = built + placed * mask1[i].astype(F32)
-    w1[...] = built.astype(BF)
-    blocks_row = [[jnp.zeros((oz, 3 * oz), BF)] * 4 for _ in range(2)]
-    for b in range(3):
-        band = jnp.zeros((oz, 3 * oz), F32)
-        for a in range(3):
-            placed = dot(dot(pick2[...], k2[a * 3 + b]).astype(BF), place2[...])
-            band = band + placed * mask2[a].astype(F32)
-        band = band.astype(BF)
-        for p in range(2):
-            blocks_row[p][b + p] = band
-    w2[...] = jnp.concatenate(
-        [jnp.concatenate(blocks_row[p], axis=1) for p in range(2)], axis=0)
-    wh[...] = (dot(dot(pick_h[...], kh[...]).astype(BF), place_h[...])
-               * mask_h[...].astype(F32)).astype(BF)
-    bias2[...] = jnp.concatenate(
-        [jnp.full((zs, WIDE), b2[o], F32) for _ in range(2) for o in range(ch)], axis=0)
-    bias_h[...] = jnp.concatenate(
-        [jnp.full((zs * 8, LANES), bh[k], F32) for k in range(aff)], axis=0)
+    oz = w1.shape[0] // 3
 
     summed = jnp.sum(stats[...], axis=0)
     summed = jnp.sum(summed, axis=2, keepdims=True)
@@ -351,45 +390,13 @@
     lax.fori_loop(0, brick_rows // 8, layer_two, 0, unroll=2)
 
 
-def compute(pixels, k1, b1, k2, b2, kh, bh, secs, tiles, rows):
-    main = pixels[0]
-    blocks, zs = main.shape[:2]
-    brick_rows = blocks * rows
-    ch, aff = b1.shape[0], bh.shape[0]
-    oz = ch * zs
-    cells = brick_rows * secs * LANES * tiles
-    k1 = jnp.transpose(k1[:, 0], (1, 3, 0, 2)).reshape(9, ch, 3)
-    k2 = jnp.transpose(k2, (2, 3, 0, 4, 1)).reshape(9, ch, 3 * ch)
-    consts = tables(zs, ch, aff)
-    vmem = pl.BlockSpec(memory_space=pltpu.VMEM)
-    smem = pl.BlockSpec(memory_space=pltpu.SMEM)
-    return pl.pallas_call(
-        functools.partial(compute_kernel, secs, tiles, rows, cells),
-        out_shape=jax.ShapeDtypeStruct((aff, zs, brick_rows, LANES), F32),
-        in_specs=[vmem] * 7 + [smem] * 3 + [vmem] * len(consts),
-        out_specs=vmem,
-        scratch_shapes=[
-            pltpu.VMEM((3 * oz, 3 * SLOTS * zs), BF),
-            pltpu.VMEM((2 * oz, 12 * oz), BF),
-            pltpu.VMEM((aff * zs * 8, 8 * oz), BF),
-            pltpu.VMEM((2 * oz, WIDE), F32),
-            pltpu.VMEM((aff * zs * 8, LANES), F32),
-            pltpu.VMEM((brick_rows + 4, SLOTS * zs, LANES), BF),
-            pltpu.VMEM((brick_rows + 2, 3 * oz, LANES), BF),
-        ],
-        compiler_params=pltpu.CompilerParams(vmem_limit_bytes=40 * 2**20),
-        name="predict",
-    )(*pixels, k1, k2, kh, b1, b2, bh, *consts)
-
-
 def per_device(
     sections_in, first_kernel, first_bias, second_kernel, second_bias, head_kernel, head_bias
 ):
     secs, tiles = lax.axis_size("sec"), lax.axis_size("tile")
-    pixels = exchange(sections_in, secs, tiles)
-    return compute(
-        pixels, first_kernel, first_bias, second_kernel, second_bias, head_kernel, head_bias,
-        secs, tiles, sections_in.shape[1])
+    return exchange(
+        sections_in, first_kernel, first_bias, second_kernel, second_bias, head_kernel,
+        head_bias, secs, tiles)
 
 
 def solution(mesh):

time: 45.7 us -> 32.6 us (0.71); the launches traced: 44.9 us -> 32.4 us
  local copies, waits for them, and re-layouts: 15.6 us -> 5.18 us
  Pallas kernels: 29.3 us -> 27.2 us
    pallas_call x1 -> x0, Pallas kernels: 11.7 us -> none  [compute(): pl.pallas_call(functools.partial(compute_kernel, secs, tiles, rows, cells...]
    unnamed x34 -> x1, local copies, waits for them, and re-layouts: 13.7 us -> 2.09 us
    pallas_call x1, Pallas kernels: 17.6 us -> 27.2 us  [exchange(): pl.pallas_call(functools.partial(exchange_kernel, secs, tiles, blocks, ro...]
    transpose x1, local copies, waits for them, and re-layouts: 0.84 us -> 1.46 us  [exchange(): k1 = jnp.transpose(k1[:, 0], (1, 3, 0, 2)).reshape(9, ch, 3)]
    reshape x2, local copies, waits for them, and re-layouts: 1.04 us -> 1.63 us  [exchange(): k2 = jnp.transpose(k2, (2, 3, 0, 4, 1)).reshape(9, ch, 3 * ch)]
where the time goes in v2:
time: 32.6 us; the launch traced here: 32.4 us
  Pallas kernels  27.2 us (83%)
  local copies, waits for them, and re-layouts  5.18 us (16%)
    pallas_call x1, Pallas kernels, exchange(): pl.pallas_call(functools.partial(exchange_kernel, secs, tiles, blocks, ro...  27.2 us
    unnamed x1, local copies, waits for them, and re-layouts  2.09 us
    reshape x2, local copies, waits for them, and re-layouts, exchange(): k2 = jnp.transpose(k2, (2, 3, 0, 4, 1)).reshape(9, ch, 3 * ch)  1.63 us
    transpose x1, local copies, waits for them, and re-layouts, exchange(): k1 = jnp.transpose(k1[:, 0], (1, 3, 0, 2)).reshape(9, ch, 3)  1.46 us

profile of v2, /device:TPU:0, one launch (start us, length us, event | category | flops | bytes accessed | tf_op | source)
XLA Modules:
  0.0 32.4 jit_solution(15525529747677431948)
XLA Ops:
  0.0 1.5 %copy.20 = bf16[3,3,12,3]{3,2,1,0:T(8,128)(2,1)} copy(bf16[3,3,12,3]{2,1,3,0:T(4,128)(2,1)} %bitcast.9) | data formatting | bytes 1296 | tf_op jit(solution)/shard_map/transpose | solution.py:271
  1.5 1.0 %reshape.8 = bf16[9,12,36]{2,0,1:T(8,128)(2,1)S(1)} reshape(bf16[3,3,12,3,12]{4,3,1,0,2:T(4,128)(2,1)} %bitcast.8) | data formatting | bytes 15552 | tf_op jit(solution)/shard_map/reshape | solution.py:272
  2.5 0.6 %copy.22.refs_2_ = bf16[9,12,36]{2,1,0:T(8,128)(2,1)} copy(bf16[9,12,36]{2,0,1:T(8,128)(2,1)S(1)} %reshape.8) | data formatting | bytes 15552 | tf_op jit(solution)/shard_map/reshape | solution.py:272
  3.1 27.2 %predict.1 = f32[3,8,64,128]{3,2,1,0:T(8,128)} custom-call(bf16[2,64,512]{2,1,0:T(8,128)(2,1)} %refs_0_.1, bf16[9,12,3]{2,1,0:T(8,128)(2,1)} %bitcast.7, bf16[9,12,36]{2,1,0:T(8,128)(2,1)} %copy.22.refs_2_, bf16[3,12]{1,0:T(4,128)(2,1)} %refs_3_.1, f32[12]{0:T(128)} %refs_4_.1, f32[12]{0:T(128)} %refs_5_.1, f32[3]{0:T(128)} %refs_6_.1, ...), custom_call_target="tpu_custom_call" | custom-call | tf_op jit(solution)/shard_map/predict/pallas_call | solution.py:280
  30.3 2.1 %copy.24 = f32[3,8,64,128]{3,2,1,0:T(8,128)} copy(f32[3,8,64,128]{3,2,1,0:T(8,128)} %predict.1) | data formatting | bytes 1572864

commit v3 on v2

--- a/solution.py
+++ b/solution.py
@@ -34,14 +34,18 @@
     for i, part in enumerate((high, mid, low)):
         built = built + part * bias_at[i].astype(F32)
     for i in range(9):
-        placed = dot(dot(pick1[...], k1[i]).astype(BF), place1[...])
+        picked = lax.dot_general(
+            pick1[...], k1[i // 3][:, i % 3, :], (((1,), (1,)), ((), ())),
+            preferred_element_type=F32)
+        placed = dot(picked.astype(BF), place1[...])
         built = built + placed * mask1[i].astype(F32)
     w1[...] = built.astype(BF)
     blocks_row = [[jnp.zeros((oz, 3 * oz), BF)] * 4 for _ in range(2)]
     for b in range(3):
         band = jnp.zeros((oz, 3 * oz), F32)
         for a in range(3):
-            placed = dot(dot(pick2[...], k2[a * 3 + b]).astype(BF), place2[...])
+            taps = jnp.concatenate([k2[:, a, b, e, :] for e in range(3)], axis=1)
+            placed = dot(dot(pick2[...], taps).astype(BF), place2[...])
             band = band + placed * mask2[a].astype(F32)
         band = band.astype(BF)
         for p in range(2):
@@ -61,11 +65,11 @@
 ):
     far = refs[:count]
     out = refs[count]
-    arrivals = refs[count + 1:count + 11]
-    main, top, bottom, stats, w1, w2, wh, bias2, bias_h, perm = arrivals
-    near = refs[count + 11:2 * count + 10] + (perm,)
-    shifted, first, load, stage, partial = refs[2 * count + 10:2 * count + 15]
-    (send_m, recv_m, send_t, recv_t, send_b, recv_b, send_s, recv_s) = refs[2 * count + 15:]
+    arrivals = refs[count + 1:count + 12]
+    main, edge, top, bottom, stats, w1, w2, wh, bias2, bias_h, perm = arrivals
+    near = refs[count + 12:2 * count + 11] + (perm,)
+    shifted, first, load, stage, partial, strip = refs[2 * count + 11:2 * count + 17]
+    (send_m, recv_m, send_e, recv_e, send_t, recv_t, send_b, recv_b, send_s, recv_s) = refs[2 * count + 17:]
     loads = [pltpu.make_async_copy(far[i], near[i], load.at[i]) for i in range(count)]
     x_ref = near[0]
     s, t = lax.axis_index("sec"), lax.axis_index("tile")
@@ -101,6 +105,9 @@
     loads[0].wait()
     sums = []
     squares = []
+    groups = staged // 16
+    strips = [jnp.zeros((16, LANES), F32)] * tiles
+    halo_lane = lax.broadcasted_iota(jnp.int32, (16, LANES), 1) < 4
     for i in range(held):
         values = x_ref[i].astype(F32)
         moved = pltpu.roll(values, 2, 1)
@@ -109,10 +116,18 @@
             moved = jnp.concatenate(
                 [moved, jnp.zeros((staged - rows, cols + LANES), F32)], axis=0)
         stage[i] = moved.astype(BF)
+        for c in range(tiles):
+            for q in range(groups):
+                kept = jnp.where(
+                    halo_lane, moved[16 * q:16 * q + 16, (c + 1) * LANES:(c + 2) * LANES], 0.0)
+                turn = 4 * (i * groups + q)
+                strips[c] = strips[c] + (pltpu.roll(kept, turn, 1) if turn else kept)
         col_sum = jnp.sum(values, axis=0, keepdims=True)
         col_square = jnp.sum(values * values, axis=0, keepdims=True)
         sums.append(sum(col_sum[:, c:c + LANES] for c in range(0, cols, LANES)))
         squares.append(sum(col_square[:, c:c + LANES] for c in range(0, cols, LANES)))
+    for c in range(tiles):
+        strip[c] = strips[c].astype(BF)
     packed = jnp.concatenate(
         sums + squares + [jnp.zeros((8 - 2 * held, LANES), F32)], axis=0)
     partial[...] = packed
@@ -167,8 +182,11 @@
     def out_pixels(act):
         def body(t2, carry):
             window = pl.ds(pl.multiple_of(t2 * LANES, LANES), WIDE)
-            act(t2 >= 0, stage.at[:, :, window], main.at[place, mine],
+            block = pl.ds(pl.multiple_of(t2 * LANES, LANES), LANES)
+            act(t2 >= 0, stage.at[:, :, block], main.at[place, mine],
                 send_m.at[t2], recv_m.at[s, place], home, t2)
+            act(t2 >= 0, strip.at[t2], edge.at[place, s],
+                send_e.at[t2], recv_e.at[s, place], home, t2)
             act(goes_up, stage.at[:, pl.ds(0, HALO_ROWS), window], bottom.at[mine],
                 send_b.at[t2], recv_b.at[s], home - 1, t2)
             act(goes_down, stage.at[:, pl.ds(staged - HALO_ROWS, HALO_ROWS), window],
@@ -185,11 +203,14 @@
 
     def in_pixels(s2, carry):
         window = pl.ds(pl.multiple_of(t * LANES, LANES), WIDE)
+        columns = pl.ds(pl.multiple_of(t * LANES, LANES), LANES)
         theirs = pl.ds(s2 * held, held)
 
         def block(k, inner):
-            arrived(s2 >= 0, stage.at[:, :, window], main.at[k, theirs],
+            arrived(s2 >= 0, stage.at[:, :, columns], main.at[k, theirs],
                     send_m.at[0], recv_m.at[s2, k], s2, s * blocks + k)
+            arrived(s2 >= 0, strip.at[t], edge.at[k, s2],
+                    send_e.at[0], recv_e.at[s2, k], s2, s * blocks + k)
             return inner
 
         lax.fori_loop(0, blocks, block, 0)
@@ -268,8 +289,8 @@
     zs = held * secs
     ch, aff = b1.shape[0], bh.shape[0]
     oz = ch * zs
-    k1 = jnp.transpose(k1[:, 0], (1, 3, 0, 2)).reshape(9, ch, 3)
-    k2 = jnp.transpose(k2, (2, 3, 0, 4, 1)).reshape(9, ch, 3 * ch)
+    k1 = jnp.transpose(k1[:, 0], (1, 2, 3, 0))
+    k2 = jnp.transpose(k2, (0, 2, 3, 4, 1))
     perm, *consts = tables(zs, ch, aff)
     operands = [x, k1, k2, kh, b1, b2, bh, *consts, perm]
     dma = pltpu.SemaphoreType.DMA
@@ -283,7 +304,8 @@
         in_specs=[hbm] * len(operands),
         out_specs=vmem,
         scratch_shapes=[
-            pltpu.VMEM((blocks, zs, staged, WIDE), BF),
+            pltpu.VMEM((blocks, zs, staged, LANES), BF),
+            pltpu.VMEM((blocks, secs, 16, LANES), BF),
             pltpu.VMEM((zs, HALO_ROWS, WIDE), BF),
             pltpu.VMEM((zs, HALO_ROWS, WIDE), BF),
             pltpu.VMEM((tiles, secs, 8, LANES), F32),
@@ -299,6 +321,8 @@
             dma((len(operands),)),
             pltpu.VMEM((held, staged, cols + LANES), BF),
             pltpu.VMEM((8, LANES), F32),
+            pltpu.VMEM((tiles, 16, LANES), BF),
+            dma((tiles,)), dma((secs, blocks)),
             dma((tiles,)), dma((secs, blocks)),
             dma((tiles,)), dma((secs,)),
             dma((tiles,)), dma((secs,)),
@@ -311,7 +335,7 @@
 
 
 def compute_kernel(
-    secs, tiles, rows, cells, main, top, bottom, stats, w1, w2, wh, bias2, bias_h, perm,
+    secs, tiles, rows, cells, main, edge, top, bottom, stats, w1, w2, wh, bias2, bias_h, perm,
     out, shifted, first,
 ):
     s, t = lax.axis_index("sec"), lax.axis_index("tile")
@@ -355,7 +379,14 @@
     for k in range(blocks):
         for q in range(staged // 16):
             row0 = k * rows + q * 16
-            ready = spread(main[k, :, q * 16:q * 16 + 16, :], row0, True)
+            halo = []
+            for z in range(zs):
+                turn = 4 * (z % held * (staged // 16) + q)
+                strip = edge[k, z // held].astype(F32)
+                halo.append(pltpu.roll(strip, LANES - turn, 1) if turn else strip)
+            halo = jnp.concatenate(halo, axis=0).astype(BF).reshape(zs, 16, LANES)
+            ready = spread(jnp.concatenate(
+                [main[k, :, q * 16:q * 16 + 16, :], halo], axis=2), row0, True)
             shifted[2 + row0:2 + row0 + step] = ready[:step]
     last = rows - 2 - (staged - HALO_ROWS)
     shifted[0:2] = spread(top[...], -2 - last, s > 0)[last:last + 2]

time: 32.6 us -> 27.2 us (0.83)
  local copies, waits for them, and re-layouts: 5.18 us -> 2.09 us
  Pallas kernels: 27.2 us -> 24.9 us
    pallas_call x1, Pallas kernels: 27.2 us -> 24.9 us  [exchange(): pl.pallas_call(functools.partial(exchange_kernel, secs, tiles, blocks, ro...]
    reshape x2 -> x0, local copies, waits for them, and re-layouts: 1.63 us -> none  [exchange(): k2 = jnp.transpose(k2, (2, 3, 0, 4, 1)).reshape(9, ch, 3 * ch)]
    transpose x1 -> x0, local copies, waits for them, and re-layouts: 1.46 us -> none  [exchange(): k1 = jnp.transpose(k1[:, 0], (1, 3, 0, 2)).reshape(9, ch, 3)]
where the time goes in v3:
time: 27.2 us; the launch traced here: 27 us
  Pallas kernels  24.9 us (92%)
  local copies, waits for them, and re-layouts  2.09 us (8%)
    pallas_call x1, Pallas kernels, exchange(): pl.pallas_call(functools.partial(exchange_kernel, secs, tiles, blocks, ro...  24.9 us
    unnamed x1, local copies, waits for them, and re-layouts  2.09 us

profile of v3, /device:TPU:0, one launch (start us, length us, event | category | flops | bytes accessed | tf_op | source)
XLA Modules:
  0.0 27.0 jit_solution(9079552317279359498)
XLA Ops:
  0.0 24.9 %predict.1 = f32[3,8,64,128]{3,2,1,0:T(8,128)} custom-call(bf16[2,64,512]{2,1,0:T(8,128)(2,1)} %refs_0_.1, bf16[3,3,3,12]{3,2,1,0:T(4,128)(2,1)} %bitcast.5, bf16[12,3,3,3,12]{4,3,2,1,0:T(4,128)(2,1)} %bitcast.4, bf16[3,12]{1,0:T(4,128)(2,1)} %refs_3_.1, f32[12]{0:T(128)} %refs_4_.1, f32[12]{0:T(128)} %refs_5_.1, f32[3]{0:T(128)} %refs_6_.1, ...), custom_call_target="tpu_custom_call" | custom-call | tf_op jit(solution)/shard_map/predict/pallas_call | solution.py:301
  25.0 2.1 %copy.21 = f32[3,8,64,128]{3,2,1,0:T(8,128)} copy(f32[3,8,64,128]{3,2,1,0:T(8,128)} %predict.1) | data formatting | bytes 1572864

commit v4 on v3

--- a/solution.py
+++ b/solution.py
@@ -68,8 +68,8 @@
     arrivals = refs[count + 1:count + 12]
     main, edge, top, bottom, stats, w1, w2, wh, bias2, bias_h, perm = arrivals
     near = refs[count + 12:2 * count + 11] + (perm,)
-    shifted, first, load, stage, partial, strip = refs[2 * count + 11:2 * count + 17]
-    (send_m, recv_m, send_e, recv_e, send_t, recv_t, send_b, recv_b, send_s, recv_s) = refs[2 * count + 17:]
+    shifted, first, load, stage, partial, strip, ends = refs[2 * count + 11:2 * count + 18]
+    (send_m, recv_m, send_e, recv_e, send_t, recv_t, send_b, recv_b, send_s, recv_s) = refs[2 * count + 18:]
     loads = [pltpu.make_async_copy(far[i], near[i], load.at[i]) for i in range(count)]
     x_ref = near[0]
     s, t = lax.axis_index("sec"), lax.axis_index("tile")
@@ -108,10 +108,13 @@
     groups = staged // 16
     strips = [jnp.zeros((16, LANES), F32)] * tiles
     halo_lane = lax.broadcasted_iota(jnp.int32, (16, LANES), 1) < 4
+    firsts, lasts = [], []
     for i in range(held):
         values = x_ref[i].astype(F32)
         moved = pltpu.roll(values, 2, 1)
         moved = jnp.concatenate([moved, moved[:, :LANES]], axis=1)
+        firsts.append(moved[:8])
+        lasts.append(moved[rows - 8:])
         if staged > rows:
             moved = jnp.concatenate(
                 [moved, jnp.zeros((staged - rows, cols + LANES), F32)], axis=0)
@@ -126,6 +129,8 @@
         col_square = jnp.sum(values * values, axis=0, keepdims=True)
         sums.append(sum(col_sum[:, c:c + LANES] for c in range(0, cols, LANES)))
         squares.append(sum(col_square[:, c:c + LANES] for c in range(0, cols, LANES)))
+    ends[0] = jnp.concatenate(firsts, axis=0).astype(BF)
+    ends[1] = jnp.concatenate(lasts, axis=0).astype(BF)
     for c in range(tiles):
         strip[c] = strips[c].astype(BF)
     packed = jnp.concatenate(
@@ -187,10 +192,10 @@
                 send_m.at[t2], recv_m.at[s, place], home, t2)
             act(t2 >= 0, strip.at[t2], edge.at[place, s],
                 send_e.at[t2], recv_e.at[s, place], home, t2)
-            act(goes_up, stage.at[:, pl.ds(0, HALO_ROWS), window], bottom.at[mine],
+            act(goes_up, ends.at[0, :, window], bottom.at[s],
                 send_b.at[t2], recv_b.at[s], home - 1, t2)
-            act(goes_down, stage.at[:, pl.ds(staged - HALO_ROWS, HALO_ROWS), window],
-                top.at[mine], send_t.at[t2], recv_t.at[s], home + 1, t2)
+            act(goes_down, ends.at[1, :, window],
+                top.at[s], send_t.at[t2], recv_t.at[s], home + 1, t2)
             return carry
 
         lax.fori_loop(0, tiles, body, 0)
@@ -214,9 +219,9 @@
             return inner
 
         lax.fori_loop(0, blocks, block, 0)
-        arrived(s > 0, stage.at[:, pl.ds(staged - HALO_ROWS, HALO_ROWS), window],
-                top.at[theirs], send_t.at[0], recv_t.at[s2], s2, s * blocks - 1)
-        arrived(s < secs - 1, stage.at[:, pl.ds(0, HALO_ROWS), window], bottom.at[theirs],
+        arrived(s > 0, ends.at[1, :, window],
+                top.at[s2], send_t.at[0], recv_t.at[s2], s2, s * blocks - 1)
+        arrived(s < secs - 1, ends.at[0, :, window], bottom.at[s2],
                 send_b.at[0], recv_b.at[s2], s2, (s + 1) * blocks)
         return carry
 
@@ -306,8 +311,8 @@
         scratch_shapes=[
             pltpu.VMEM((blocks, zs, staged, LANES), BF),
             pltpu.VMEM((blocks, secs, 16, LANES), BF),
-            pltpu.VMEM((zs, HALO_ROWS, WIDE), BF),
-            pltpu.VMEM((zs, HALO_ROWS, WIDE), BF),
+            pltpu.VMEM((secs, 8 * held, WIDE), BF),
+            pltpu.VMEM((secs, 8 * held, WIDE), BF),
             pltpu.VMEM((tiles, secs, 8, LANES), F32),
             pltpu.VMEM((3 * oz, 3 * SLOTS * zs), BF),
             pltpu.VMEM((2 * oz, 12 * oz), BF),
@@ -322,6 +327,7 @@
             pltpu.VMEM((held, staged, cols + LANES), BF),
             pltpu.VMEM((8, LANES), F32),
             pltpu.VMEM((tiles, 16, LANES), BF),
+            pltpu.VMEM((2, 8 * held, cols + LANES), BF),
             dma((tiles,)), dma((secs, blocks)),
             dma((tiles,)), dma((secs, blocks)),
             dma((tiles,)), dma((secs,)),
@@ -388,9 +394,14 @@
             ready = spread(jnp.concatenate(
                 [main[k, :, q * 16:q * 16 + 16, :], halo], axis=2), row0, True)
             shifted[2 + row0:2 + row0 + step] = ready[:step]
-    last = rows - 2 - (staged - HALO_ROWS)
-    shifted[0:2] = spread(top[...], -2 - last, s > 0)[last:last + 2]
-    shifted[2 + brick_rows:4 + brick_rows] = spread(bottom[...], brick_rows, s < secs - 1)[0:2]
+
+    def filled(halo_rows):
+        held_rows = halo_rows[...].astype(F32).reshape(zs, 8, WIDE)
+        return jnp.concatenate([held_rows, jnp.zeros_like(held_rows)], axis=1).astype(BF)
+
+    shifted[0:2] = spread(filled(top), -8, s > 0)[6:8]
+    shifted[2 + brick_rows:4 + brick_rows] = spread(
+        filled(bottom), brick_rows, s < secs - 1)[0:2]
 
     depth1 = w1.shape[1]
 

time: 27.2 us -> 26.2 us (0.963)
  Pallas kernels: 24.9 us -> 23.9 us
    pallas_call x1, Pallas kernels: 24.9 us -> 23.9 us  [exchange(): pl.pallas_call(functools.partial(exchange_kernel, secs, tiles, blocks, ro...]
where the time goes in v4:
time: 26.2 us; the launch traced here: 26 us
  Pallas kernels  23.9 us (91%)
  local copies, waits for them, and re-layouts  2.09 us (8%)
    pallas_call x1, Pallas kernels, exchange(): pl.pallas_call(functools.partial(exchange_kernel, secs, tiles, blocks, ro...  23.9 us
    unnamed x1, local copies, waits for them, and re-layouts  2.09 us

profile of v4, /device:TPU:0, one launch (start us, length us, event | category | flops | bytes accessed | tf_op | source)
XLA Modules:
  0.0 26.0 jit_solution(17059659993789373584)
XLA Ops:
  0.0 23.9 %predict.1 = f32[3,8,64,128]{3,2,1,0:T(8,128)} custom-call(bf16[2,64,512]{2,1,0:T(8,128)(2,1)} %refs_0_.1, bf16[3,3,3,12]{3,2,1,0:T(4,128)(2,1)} %bitcast.5, bf16[12,3,3,3,12]{4,3,2,1,0:T(4,128)(2,1)} %bitcast.4, bf16[3,12]{1,0:T(4,128)(2,1)} %refs_3_.1, f32[12]{0:T(128)} %refs_4_.1, f32[12]{0:T(128)} %refs_5_.1, f32[3]{0:T(128)} %refs_6_.1, ...), custom_call_target="tpu_custom_call" | custom-call | tf_op jit(solution)/shard_map/predict/pallas_call | solution.py:306
  23.9 2.1 %copy.21 = f32[3,8,64,128]{3,2,1,0:T(8,128)} copy(f32[3,8,64,128]{3,2,1,0:T(8,128)} %predict.1) | data formatting | bytes 1572864
